TPU v7x, 256 devices: a whole 4x4x8 slice. The times are simulated.
256 devices in a mesh: cfg: 2 (over y_lo), req: 8 (over x, core), seq: 16 (over z, y_hi).
Axes of the slice: x: 4, y: 4 (y_hi: 2, y_lo: 2; y = y_hi * 2 + y_lo), z: 8, core: 2. Of those that a mesh axis runs over, the one named last changes fastest.
Arguments:
- image_hidden: bfloat16 [2, 8, 2048, 1536], P('cfg', 'req', 'seq'), may hold values from -6 to 6
- text_hidden: bfloat16 [2, 8, 160, 1536], P('cfg', 'req', 'seq'), may hold values from -6 to 6
- modulation: float32 [2, 8, 10, 1536], P('cfg', 'req'), may hold values from -3 to 3
- attn_weight: bfloat16 [1536, 5120], P(None, 'seq'), may hold values from -8 to 8
- proj_weight: bfloat16 [1024, 1536], replicated, may hold values from -0.1875 to 0.1875
- mlp_in_weight: bfloat16 [1536, 6144], P(None, 'seq'), may hold values from -0.15625 to 0.15625
- mlp_out_weight: bfloat16 [6144, 1536], P('seq'), may hold values from -0.078125 to 0.078125
- final_weight: bfloat16 [64, 1536], replicated, may hold values from -0.15625 to 0.15625
- latents: float32 [8, 64, 2048], P('req', 'cfg', 'seq'), may hold values from -6 to 6
- guidance: float32 [8], P('req'), may hold values from 3 to 7
- text_lengths: int32 [2, 8], P('cfg', 'req'), may hold values from 1 to 154, 693 in all within a row
- step_index: int32 [8], P('req'), may hold values from 0 to 27
- step_count: int32 [8], P('req'), may hold values from 1 to 3
Outputs:
- velocity: float32 [8, 64, 2048], P('req', 'cfg', 'seq')
- new_latents: float32 [8, 64, 2048], P('req', 'cfg', 'seq')
All inputs are finite; a program needn't handle non-finite values. No bound on the sum of `text_lengths` on one device may be relied on, other than what follows from the above.
Results may differ from a plain program's by a relative error of at most 0.017.
Values may be sent and summed in bfloat16 or wider, within the bound.
No kernel may reach another device: no remote copies, remote signals or barrier semaphores. Data moves between devices by JAX's collectives and lax.ppermute only.
A program may use at most 128 MiB of HBM per device.

v0:
```python
import jax
import jax.numpy as jnp
from jax import lax
from jax.sharding import PartitionSpec as P

HEADS = 16
HEAD = 64
STEPS = 28
EPS_NORM = 1e-06


def partner(value, axis, distance):
    mask = 2**distance
    pairs = [(source, source ^ mask) for source in range(lax.axis_size(axis))]
    return lax.ppermute(value, axis, pairs)


def modulate(rows_in, scale_row, shift_row):
    values = rows_in.astype(jnp.float32)
    center = jnp.mean(values, axis=-1, keepdims=True)
    spread = jnp.mean(jnp.square(values - center), axis=-1, keepdims=True)
    return (
        (values - center) * lax.rsqrt(spread + EPS_NORM) * (1.0 + scale_row) + shift_row
    ).astype(jnp.bfloat16)


def sigma_of(index):
    remain = 1.0 - index.astype(jnp.float32) / STEPS
    return 3.0 * remain / (1.0 + 2.0 * remain)


def split_columns(weight_piece):
    width_in = weight_piece.shape[0]
    head_count = weight_piece.shape[1] // (5 * HEAD)
    shaped = weight_piece.reshape(width_in, head_count, 5, HEAD)
    image_cols = shaped[:, :, 0:3, :].reshape(width_in, head_count * 3 * HEAD)
    text_cols = shaped[:, :, 3:5, :].reshape(width_in, head_count * 2 * HEAD)
    return (image_cols, text_cols)


def local(
    image_hidden,
    text_hidden,
    modulation,
    attn_weight,
    proj_weight,
    mlp_in_weight,
    mlp_out_weight,
    final_weight,
    latents,
    guidance,
    text_lengths,
    step_index,
    step_count,
):
    seq_size = lax.axis_size("seq")
    local_heads = HEADS // seq_size
    image_rows = image_hidden[0, 0]
    text_rows = text_hidden[0, 0]
    mod_rows = modulation[0, 0]
    local_rows = image_rows.shape[0]
    image_total = local_rows * seq_size
    text_total = text_rows.shape[0] * seq_size
    image_norm = modulate(image_rows, mod_rows[1], mod_rows[0])
    text_norm = modulate(text_rows, mod_rows[4], mod_rows[3])
    image_cols, text_cols = split_columns(lax.all_gather(attn_weight, "seq", axis=1, tiled=True))
    image_part = jnp.dot(image_norm, image_cols, preferred_element_type=jnp.float32).astype(
        jnp.bfloat16
    )
    text_part = jnp.dot(text_norm, text_cols, preferred_element_type=jnp.float32).astype(
        jnp.bfloat16
    )
    image_qkv = image_part
    text_kv = text_part
    image_qkv, text_kv = (
        lax.all_to_all(image_qkv, "seq", split_axis=1, concat_axis=0, tiled=True),
        lax.all_to_all(text_kv, "seq", split_axis=1, concat_axis=0, tiled=True),
    )
    image_qkv = image_qkv.reshape(image_total, local_heads, 3, HEAD)
    text_kv = text_kv.reshape(text_total, local_heads, 2, HEAD)
    keys_all = jnp.concatenate([image_qkv[:, :, 1], text_kv[:, :, 0]], axis=0)
    values_all = jnp.concatenate([image_qkv[:, :, 2], text_kv[:, :, 1]], axis=0)
    slots = jnp.arange(text_total, dtype=jnp.int32)
    valid = jnp.concatenate([jnp.ones((image_total,), dtype=bool), slots < text_lengths[0, 0]])
    block_rows = local_rows
    while block_rows < 512 and image_total % (block_rows * 2) == 0:
        block_rows = block_rows * 2
    block_total = image_total // block_rows
    query_blocks = image_qkv[:, :, 0].reshape(block_total, block_rows, local_heads, HEAD)

    def attend(query_block):
        scores = jnp.einsum(
            "qhe,khe->hqk", query_block, keys_all, preferred_element_type=jnp.float32
        ) * HEAD ** (-0.5)
        scores = jnp.where(valid[None, None, :], scores, -1e30)
        row_max = jnp.max(scores, axis=2, keepdims=True)
        weights = jnp.exp(scores - row_max)
        total = jnp.sum(weights, axis=2, keepdims=True)
        probs = weights.astype(jnp.bfloat16)
        mixed = (
            jnp.einsum("hqk,khe->hqe", probs, values_all, preferred_element_type=jnp.float32)
            / total
        )
        return jnp.transpose(mixed.astype(jnp.bfloat16), (1, 0, 2))

    attended = lax.map(attend, query_blocks).reshape(image_total, local_heads * HEAD)
    attended = lax.all_to_all(attended, "seq", split_axis=0, concat_axis=1, tiled=True)
    hidden = image_rows.astype(jnp.float32) + mod_rows[2] * jnp.dot(
        attended, proj_weight, preferred_element_type=jnp.float32
    )
    mlp_norm = modulate(hidden, mod_rows[8], mod_rows[7])
    mlp_all = lax.all_gather(mlp_norm, "seq", axis=0, tiled=True)
    inner = jax.nn.gelu(
        jnp.dot(mlp_all, mlp_in_weight, preferred_element_type=jnp.float32), approximate=True
    ).astype(jnp.bfloat16)
    mlp_out = lax.psum_scatter(
        jnp.dot(inner, mlp_out_weight, preferred_element_type=jnp.float32).astype(jnp.bfloat16),
        "seq",
        scatter_dimension=0,
        tiled=True,
    ).astype(jnp.float32)
    block_out = hidden + mod_rows[9] * mlp_out
    final_norm = modulate(block_out, mod_rows[6], mod_rows[5])
    own_vel = lax.dot_general(
        final_weight, final_norm, (((1,), (1,)), ((), ())), preferred_element_type=jnp.float32
    )
    partner_vel = partner(own_vel.astype(jnp.bfloat16), "cfg", 0).astype(own_vel.dtype)
    leading = lax.axis_index("cfg") == 0
    cond_vel = jnp.where(leading, own_vel, partner_vel)
    uncond_vel = jnp.where(leading, partner_vel, own_vel)
    guided = uncond_vel + guidance[0] * (cond_vel - uncond_vel)
    cond_sq, guided_sq = lax.psum((jnp.sum(cond_vel * cond_vel), jnp.sum(guided * guided)), "seq")
    entries = own_vel.shape[0] * image_total
    rms_cond = jnp.sqrt(cond_sq / entries + EPS_NORM)
    rms_guided = jnp.sqrt(guided_sq / entries + EPS_NORM)
    result_vel = 0.7 * (guided * (rms_cond / rms_guided)) + 0.3 * guided
    channel_half = latents.shape[1]
    channel_start = lax.axis_index("cfg") * channel_half
    own_channels = lax.dynamic_slice_in_dim(result_vel, channel_start, channel_half, 0)
    next_index = jnp.minimum(step_index[0] + step_count[0], STEPS)
    step_size = sigma_of(next_index) - sigma_of(step_index[0])
    moved = latents[0] + step_size * own_channels
    return (own_channels[None], moved[None])


def solution(mesh):
    in_specs = (
        P("cfg", "req", "seq", None),
        P("cfg", "req", "seq", None),
        P("cfg", "req", None, None),
        P(None, "seq"),
        P(),
        P(None, "seq"),
        P("seq", None),
        P(),
        P("req", "cfg", "seq"),
        P("req"),
        P("cfg", "req"),
        P("req"),
        P("req"),
    )
    out_specs = (P("req", "cfg", "seq"), P("req", "cfg", "seq"))
    return jax.shard_map(local, mesh=mesh, in_specs=in_specs, out_specs=out_specs, check_vma=False)
```

profile of v0, /device:TPU:2, one launch (start us, length us, event | category | flops | bytes accessed | tf_op | source)
XLA Modules:
  0.0 735.5 jit_solution(12399066604961495987)
XLA Ops:
  10.6 1.6 slice_reduce_fusion.2
  16.3 210.6 %all-gather.3.cloned.1.call-done = bf16[1536,5120]{0,1:T(8,128)(2,1)} async-done(((bf16[1536,320]{0,1:T(8,128)(2,1)}), bf16[1536,5120]{0,1:T(8,128)(2,1)}) %all-gather.3.cloned.1.call-update) | async-done | bytes 15728656 | tf_op jit(solution)/shard_map/all_gather | solution.py:66
  226.9 8.3 %slice.78 = bf16[1536,16,3,64]{0,3,2,1:T(8,128)(2,1)} slice(bf16[1536,16,5,64]{0,3,2,1:T(8,128)(2,1)} %bitcast.100), slice={[0:1536], [0:16], [0:3], [0:64]} | slice | bytes 18874368 | tf_op jit(solution)/shard_map/slice | solution.py:36
  235.2 3.5 slice.81
  238.8 1.7 convolution_convert_fusion.2
  241.2 4.5 all-to-all-start.1
  245.8 7.8 %convolution_convert_fusion.1 = bf16[128,3072]{1,0:T(8,128)(2,1)} fusion(bf16[1536,3072]{0,1:T(8,128)(2,1)} %bitcast.98, bf16[1,1,128,1536]{3,2,1,0:T(8,128)(2,1)S(1)} %copy-done.3, f32[1536]{0:T(1024)} %get-tuple-element.58, f32[1536]{0:T(1024)} %get-tuple-element.59, f32[128]{0:T(128)} %add_rsqrt_fusion.3, f32[128]{0:T(128)} %copy-done.12), kind=kOutput, calls=%fused_computation.18 | convolution fusion | flops 1209532416 | bytes 10630144 | tf_op jit(solution)/shard_map/dot_general | solution.py:67
  253.6 2.3 copy.24
  256.4 9.1 %all-to-all-start = ((bf16[128,16,192]{0,2,1:T(8,128)(2,1)}), bf16[128,16,192]{0,2,1:T(8,128)(2,1)}, u32[]{:S(2)}, u32[]{:S(2)}) async-start(bf16[128,16,192]{0,2,1:T(8,128)(2,1)} %bitcast.102), calls=%async_computation | async-start | bytes 1572864 | tf_op jit(solution)/shard_map/all_to_all | solution.py:76
  267.5 21.1 %all-to-all-done = bf16[128,16,192]{0,2,1:T(8,128)(2,1)} async-done(((bf16[128,16,192]{0,2,1:T(8,128)(2,1)}), bf16[128,16,192]{0,2,1:T(8,128)(2,1)}, u32[]{:S(2)}, u32[]{:S(2)}) %all-to-all-start) | async-done | bytes 786464 | tf_op jit(solution)/shard_map/all_to_all | solution.py:76
  288.6 2.5 copy.25
  291.2 2.1 reshape.237
  293.3 2.0 slice_bitcast_fusion
  297.2 1.8 pad_maximum_fusion
  299.0 17.0 %while.10 = (s32[]{:T(128)}, bf16[4,512,1,64]{1,3,2,0:T(8,128)(2,1)}, pred[2208]{0:T(1024)(128)(4,1)S(1)}, bf16[4,512,1,64]{1,3,2,0:T(8,128)(2,1)}, bf16[2208,1,...) while((s32[]{:T(128)}, bf16[4,512,1,64]{1,3,2,0:T(8,128)(2,1)}, ...), condition=%wide.region_7.8_spmd, body=%wide.region_4.7_spmd.sunk | while | flops 297384960 | bytes 15406345 | solution.py:106
  299.0 1.9 fusion.95
  301.8 1.4 fusion.97
  303.3 1.8 fusion.95
  306.1 1.4 fusion.97
  307.5 1.8 fusion.95
  310.3 1.4 fusion.97
  311.8 1.8 fusion.95
  314.6 1.4 fusion.97
  319.0 16.4 %all_to_all.51 = bf16[16,128,64]{1,2,0:T(8,128)(2,1)S(1)} all-to-all(bf16[16,128,64]{1,2,0:T(8,128)(2,1)S(1)} %copy.31), channel_id=1, replica_groups=mesh['cfg'=2,'req'=8,'seq'=16] {'seq'}, dimensions={0} | all-to-all | bytes 524288 | tf_op jit(solution)/shard_map/all_to_all | solution.py:107
  335.4 1.7 fusion.76
  339.3 110.8 %all-gather.5.cloned.1.call-done = bf16[2048,1536]{1,0:T(8,128)(2,1)} async-done(((bf16[128,1536]{1,0:T(8,128)(2,1)}), bf16[2048,1536]{1,0:T(8,128)(2,1)}) %all-gather.5.cloned.1.call-update) | async-done | bytes 6291472 | tf_op jit(solution)/shard_map/all_gather | solution.py:112
  450.1 11.5 %convolution_convert_fusion = bf16[2048,1536]{1,0:T(8,128)(2,1)} fusion(bf16[384,1536]{1,0:T(8,128)(2,1)} %param.21, bf16[2048,1536]{1,0:T(8,128)(2,1)} %all-gather.5.cloned.1.call-done, bf16[1536,384]{1,0:T(8,128)(2,1)} %param.20), kind=kOutput, calls=%fused_computation.16 | convolution fusion | flops 4842061824 | bytes 14942208 | tf_op jit(solution)/shard_map/dot_general | solution.py:117
  461.6 216.7 %reduce-scatter.2.cloned.1.call-done = bf16[128,1536]{1,0:T(8,128)(2,1)} async-done(((bf16[2048,1536]{1,0:T(8,128)(2,1)}), bf16[128,1536]{1,0:T(8,128)(2,1)}) %reduce-scatter.2.cloned.1.call-update) | async-done | bytes 393232 | tf_op jit(solution)/shard_map/reduce_scatter | solution.py:116
  678.3 1.4 fusion.54
  679.8 1.5 multiply_reduce_fusion
  681.3 1.6 fusion.77
  687.3 39.7 %all-reduce.1 = (f32[]{:T(128)}, f32[]{:T(128)}) all-reduce(f32[]{:T(128)} %get-tuple-element.86, f32[]{:T(128)} %get-tuple-element.77), channel_id=1, replica_groups=mesh['cfg'=2,'req'=8,'seq'=16] {'seq'}, use_global_device_ids=true, to_apply=%region_14.15 | all-reduce | flops 2 | bytes 16 | tf_op jit(solution)/shard_map/psum | solution.py:132
  (84 shorter events, 23.8 us)
Async XLA Ops:
  7.2 328.3 %copy-start = (bf16[1024,1536]{1,0:T(8,128)(2,1)S(1)}, bf16[1024,1536]{1,0:T(8,128)(2,1)}, u32[]{:S(2)}) copy-start(bf16[1024,1536]{1,0:T(8,128)(2,1)} %param.19) | copy-start | bytes 9437188
  7.2 219.8 %all-gather.3.cloned.1.call-start = ((), (), s32[]{:S(2)}) async-start(), calls=%async_computation.4 | async-start | bytes 16711680 | tf_op jit(solution)/shard_map/all_gather | solution.py:66
  9.0 0.6 copy-start.13
  13.4 0.6 copy-start.12
  235.2 3.5 copy-start.4
  235.2 3.5 copy-start.7
  235.2 3.6 copy-start.8
  235.2 3.6 copy-start.14
  235.2 3.6 copy-start.15
  238.8 6.9 copy-start.3
  241.2 15.1 %all-to-all-start.1 = ((bf16[10,16,128]{2,0,1:T(8,128)(2,1)}), bf16[10,16,128]{2,0,1:T(8,128)(2,1)}, u32[]{:S(2)}, u32[]{:S(2)}) async-start(bf16[10,16,128]{2,0,1:T(8,128)(2,1)} %copy.26), calls=%async_computation.1 | async-start | bytes 131072 | tf_op jit(solution)/shard_map/all_to_all | solution.py:77
  256.4 32.3 %all-to-all-start = ((bf16[128,16,192]{0,2,1:T(8,128)(2,1)}), bf16[128,16,192]{0,2,1:T(8,128)(2,1)}, u32[]{:S(2)}, u32[]{:S(2)}) async-start(bf16[128,16,192]{0,2,1:T(8,128)(2,1)} %bitcast.102), calls=%async_computation | async-start | bytes 1572864 | tf_op jit(solution)/shard_map/all_to_all | solution.py:76
  265.5 184.6 %all-gather.5.cloned.1.call-start = ((), (), s32[]{:S(2)}) async-start(), calls=%async_computation.5 | async-start | bytes 6684672 | tf_op jit(solution)/shard_map/all_gather | solution.py:112
  299.0 36.4 %copy-start.6 = (f32[1536]{0:T(1024)S(1)}, f32[1536]{0:T(1024)}, u32[]{:S(2)}) copy-start(f32[1536]{0:T(1024)} %get-tuple-element.60) | copy-start | bytes 18436
  300.8 1.0 copy-start.2
  305.1 1.0 copy-start.2
  309.4 1.0 copy-start.2
  313.6 1.0 copy-start.2
  318.0 20.1 %copy-start.5 = (f32[1536]{0:T(1024)S(1)}, f32[1536]{0:T(1024)}, u32[]{:S(2)}) copy-start(f32[1536]{0:T(1024)} %get-tuple-element.55) | copy-start | bytes 18436
  337.1 0.9 copy-start.1
  339.1 339.3 %reduce-scatter.2.cloned.1.call-start = ((), (), s32[]{:S(2)}) async-start(), calls=%async_computation.6 | async-start | bytes 6684672 | tf_op jit(solution)/shard_map/reduce_scatter | solution.py:116
  461.6 219.7 %copy-start.10 = (f32[1536]{0:T(1024)S(1)}, f32[1536]{0:T(1024)}, u32[]{:S(2)}) copy-start(f32[1536]{0:T(1024)} %get-tuple-element.61) | copy-start | bytes 18436
  461.6 219.7 %copy-start.11 = (f32[1536]{0:T(1024)S(1)}, f32[1536]{0:T(1024)}, u32[]{:S(2)}) copy-start(f32[1536]{0:T(1024)} %get-tuple-element.62) | copy-start | bytes 18436
  461.6 219.7 %copy-start.16 = (bf16[64,1536]{1,0:T(8,128)(2,1)S(1)}, bf16[64,1536]{1,0:T(8,128)(2,1)}, u32[]{:S(2)}) copy-start(bf16[64,1536]{1,0:T(8,128)(2,1)} %param.22) | copy-start | bytes 589828
  461.6 266.8 %copy-start.9 = (f32[1,32,128]{2,1,0:T(8,128)S(1)}, f32[1,32,128]{2,1,0:T(8,128)}, u32[]{:S(2)}) copy-start(f32[1,32,128]{2,1,0:T(8,128)} %param.23) | copy-start | bytes 49156
  682.9 3.8 collective-permute-start
Sparse Core Ops, SparseCore 0:
  10.6 216.2 all-gather.2
  339.2 110.8 all-gather.4
  461.7 216.5 reduce-scatter.1
where the time goes:
time: 737 us; the launch traced here: 736 us
  waiting for transfers between devices  562 us (76%)
  blocking collectives  56.1 us (8%)
  matrix products  37.5 us (5%)
  local copies, waits for them, and re-layouts  30.5 us (4%)
  between operations  18.1 us (2%)
  other arithmetic  17.1 us (2%)
  starting transfers between devices  14.7 us (2%)
    reduce_scatter x1, waiting for transfers between devices, local(): lax.psum_scatter(jnp.dot(inner, mlp_out_weight, preferred_element_type=jn...  217 us
    all_gather x1, waiting for transfers between devices, local(): lax.all_gather(attn_weight, 'seq', axis=1, tiled=True)  211 us
    all_gather x1, waiting for transfers between devices, local(): mlp_all = lax.all_gather(mlp_norm, 'seq', axis=0, tiled=True)  111 us
    psum x1, blocking collectives, local(): lax.psum((jnp.sum(cond_vel * cond_vel), jnp.sum(guided * guided)), 'seq')  39.7 us
    all_to_all x1, waiting for transfers between devices, local(): lax.all_to_all(image_qkv, 'seq', split_axis=1, concat_axis=0, tiled=True)  21.1 us
    all_to_all x1, blocking collectives, local(): lax.all_to_all(attended, 'seq', split_axis=0, concat_axis=1, tiled=True)  16.4 us
  transfers between devices with their start and end apart: 6, of which 6 were waited for; matrix products, arithmetic and copies ran while one was open for 3% of the time, Pallas kernels for 0%

commit v1 on v0

--- a/solution.py
+++ b/solution.py
@@ -7,6 +7,11 @@
 HEAD = 64
 STEPS = 28
 EPS_NORM = 1e-06
+
+
+def gather_over(array, axis, along):
+    sent = jnp.stack([array] * lax.axis_size(axis))
+    return jnp.concatenate(lax.all_to_all(sent, axis, 0, 0), axis=along)
 
 
 def partner(value, axis, distance):
@@ -109,7 +114,7 @@
         attended, proj_weight, preferred_element_type=jnp.float32
     )
     mlp_norm = modulate(hidden, mod_rows[8], mod_rows[7])
-    mlp_all = lax.all_gather(mlp_norm, "seq", axis=0, tiled=True)
+    mlp_all = gather_over(mlp_norm, "seq", 0)
     inner = jax.nn.gelu(
         jnp.dot(mlp_all, mlp_in_weight, preferred_element_type=jnp.float32), approximate=True
     ).astype(jnp.bfloat16)

time: 737 us -> 768 us (1.042)
  blocking collectives: 56.1 us -> 200 us
  waiting for transfers between devices: 562 us -> 450 us
    all_to_all x0 -> x1, blocking collectives: none -> 144 us  [gather_over(): return jnp.concatenate(lax.all_to_all(sent, axis, 0, 0), axis=along)]
    all_gather x1 -> x0, waiting for transfers between devices: 111 us -> none  [local(): mlp_all = lax.all_gather(mlp_norm, 'seq', axis=0, tiled=True)]
  transfers between devices with their start and end apart: 6 -> 5, of which waited for: 6 -> 5; matrix products, arithmetic and copies ran while one was open for 3% -> 2% of each run, Pallas kernels for 0% -> 0%
where the time goes in v1:
time: 768 us; the launch traced here: 767 us
  waiting for transfers between devices  450 us (59%)
  blocking collectives  200 us (26%)
  matrix products  37.8 us (5%)
  local copies, waits for them, and re-layouts  30 us (4%)
  between operations  18.4 us (2%)
  other arithmetic  16.3 us (2%)
  starting transfers between devices  14.4 us (2%)
    reduce_scatter x1, waiting for transfers between devices, local(): lax.psum_scatter(jnp.dot(inner, mlp_out_weight, preferred_element_type=jn...  216 us
    all_gather x1, waiting for transfers between devices, local(): lax.all_gather(attn_weight, 'seq', axis=1, tiled=True)  211 us
    all_to_all x1, blocking collectives, gather_over(): return jnp.concatenate(lax.all_to_all(sent, axis, 0, 0), axis=along)  144 us
    psum x1, blocking collectives, local(): lax.psum((jnp.sum(cond_vel * cond_vel), jnp.sum(guided * guided)), 'seq')  39.7 us
    all_to_all x1, waiting for transfers between devices, local(): lax.all_to_all(image_qkv, 'seq', split_axis=1, concat_axis=0, tiled=True)  21.1 us
    all_to_all x1, blocking collectives, local(): lax.all_to_all(attended, 'seq', split_axis=0, concat_axis=1, tiled=True)  16.4 us
  transfers between devices with their start and end apart: 5, of which 5 were waited for; matrix products, arithmetic and copies ran while one was open for 2% of the time, Pallas kernels for 0%

profile of v1, /device:TPU:2, one launch (start us, length us, event | category | flops | bytes accessed | tf_op | source)
XLA Modules:
  0.0 767.0 jit_solution(16850300318109841181)
XLA Ops:
  10.6 1.6 slice_reduce_fusion.2
  16.3 210.6 %all-gather.2.cloned.1.call-done = bf16[1536,5120]{0,1:T(8,128)(2,1)} async-done(((bf16[1536,320]{0,1:T(8,128)(2,1)}), bf16[1536,5120]{0,1:T(8,128)(2,1)}) %all-gather.2.cloned.1.call-update) | async-done | bytes 15728656 | tf_op jit(solution)/shard_map/all_gather | solution.py:71
  226.9 8.3 %slice.78 = bf16[1536,16,3,64]{0,3,2,1:T(8,128)(2,1)} slice(bf16[1536,16,5,64]{0,3,2,1:T(8,128)(2,1)} %bitcast.101), slice={[0:1536], [0:16], [0:3], [0:64]} | slice | bytes 18874368 | tf_op jit(solution)/shard_map/slice | solution.py:41
  235.2 3.5 slice.81
  238.8 1.7 convolution_convert_fusion.2
  241.2 4.5 all-to-all-start.1
  245.8 7.8 %convolution_convert_fusion.1 = bf16[128,3072]{1,0:T(8,128)(2,1)} fusion(bf16[1536,3072]{0,1:T(8,128)(2,1)} %bitcast.99, bf16[1,1,128,1536]{3,2,1,0:T(8,128)(2,1)S(1)} %copy-done.3, f32[1536]{0:T(1024)} %get-tuple-element.58, f32[1536]{0:T(1024)} %get-tuple-element.59, f32[128]{0:T(128)} %add_rsqrt_fusion.3, f32[128]{0:T(128)} %copy-done.12), kind=kOutput, calls=%fused_computation.18 | convolution fusion | flops 1209532416 | bytes 10630144 | tf_op jit(solution)/shard_map/dot_general | solution.py:72
  253.6 2.3 copy.24
  256.4 9.1 %all-to-all-start = ((bf16[128,16,192]{0,2,1:T(8,128)(2,1)}), bf16[128,16,192]{0,2,1:T(8,128)(2,1)}, u32[]{:S(2)}, u32[]{:S(2)}) async-start(bf16[128,16,192]{0,2,1:T(8,128)(2,1)} %bitcast.104), calls=%async_computation | async-start | bytes 1572864 | tf_op jit(solution)/shard_map/all_to_all | solution.py:81
  267.5 21.1 %all-to-all-done = bf16[128,16,192]{0,2,1:T(8,128)(2,1)} async-done(((bf16[128,16,192]{0,2,1:T(8,128)(2,1)}), bf16[128,16,192]{0,2,1:T(8,128)(2,1)}, u32[]{:S(2)}, u32[]{:S(2)}) %all-to-all-start) | async-done | bytes 786464 | tf_op jit(solution)/shard_map/all_to_all | solution.py:81
  288.6 2.5 copy.25
  291.2 2.1 reshape.242
  293.3 2.0 slice_bitcast_fusion
  297.2 1.8 pad_maximum_fusion
  299.0 16.1 %while.10 = (s32[]{:T(128)}, bf16[4,512,1,64]{1,3,2,0:T(8,128)(2,1)}, pred[2208]{0:T(1024)(128)(4,1)S(1)}, bf16[4,512,1,64]{1,3,2,0:T(8,128)(2,1)}, bf16[2208,1,...) while((s32[]{:T(128)}, bf16[4,512,1,64]{1,3,2,0:T(8,128)(2,1)}, ...), condition=%wide.region_7.8_spmd, body=%wide.region_4.7_spmd.sunk | while | flops 297384960 | bytes 15406345 | solution.py:111
  299.0 1.9 fusion.95
  301.6 1.5 fusion.97
  303.0 1.9 fusion.95
  305.6 1.5 fusion.97
  307.0 1.9 fusion.95
  309.6 1.4 fusion.97
  311.1 1.9 fusion.95
  313.6 1.4 fusion.97
  318.1 16.4 %all_to_all.56 = bf16[16,128,64]{1,2,0:T(8,128)(2,1)S(1)} all-to-all(bf16[16,128,64]{1,2,0:T(8,128)(2,1)S(1)} %copy.31), channel_id=1, replica_groups=mesh['cfg'=2,'req'=8,'seq'=16] {'seq'}, dimensions={0} | all-to-all | bytes 524288 | tf_op jit(solution)/shard_map/all_to_all | solution.py:112
  334.5 1.7 fusion.76
  337.9 144.4 %all_to_all.57 = bf16[16,128,1536]{2,1,0:T(8,128)(2,1)} all-to-all(bf16[16,128,1536]{2,1,0:T(8,128)(2,1)S(1)} %stack.2), channel_id=1, replica_groups=mesh['cfg'=2,'req'=8,'seq'=16] {'seq'}, dimensions={0} | all-to-all | bytes 12582912 | tf_op jit(solution)/shard_map/all_to_all | solution.py:14
  482.3 11.6 %convolution_convert_fusion = bf16[2048,1536]{1,0:T(8,128)(2,1)} fusion(bf16[384,1536]{1,0:T(8,128)(2,1)} %param.21, bf16[2048,1536]{1,0:T(8,128)(2,1)} %bitcast.103, bf16[1536,384]{1,0:T(8,128)(2,1)} %param.20), kind=kOutput, calls=%fused_computation.16 | convolution fusion | flops 4842061824 | bytes 14942208 | tf_op jit(solution)/shard_map/dot_general | solution.py:122
  493.9 215.5 %reduce-scatter.2.cloned.1.call-done = bf16[128,1536]{1,0:T(8,128)(2,1)} async-done(((bf16[2048,1536]{1,0:T(8,128)(2,1)}), bf16[128,1536]{1,0:T(8,128)(2,1)}) %reduce-scatter.2.cloned.1.call-update) | async-done | bytes 393232 | tf_op jit(solution)/shard_map/reduce_scatter | solution.py:121
  709.4 1.4 fusion.54
  710.9 1.5 multiply_reduce_fusion
  712.4 1.6 fusion.77
  718.4 39.7 %all-reduce.1 = (f32[]{:T(128)}, f32[]{:T(128)}) all-reduce(f32[]{:T(128)} %get-tuple-element.86, f32[]{:T(128)} %get-tuple-element.77), channel_id=1, replica_groups=mesh['cfg'=2,'req'=8,'seq'=16] {'seq'}, use_global_device_ids=true, to_apply=%region_14.15 | all-reduce | flops 2 | bytes 16 | tf_op jit(solution)/shard_map/psum | solution.py:137
  (83 shorter events, 22.3 us)
Async XLA Ops:
  7.2 327.3 %copy-start = (bf16[1024,1536]{1,0:T(8,128)(2,1)S(1)}, bf16[1024,1536]{1,0:T(8,128)(2,1)}, u32[]{:S(2)}) copy-start(bf16[1024,1536]{1,0:T(8,128)(2,1)} %param.19) | copy-start | bytes 9437188
  7.2 219.8 %all-gather.2.cloned.1.call-start = ((), (), s32[]{:S(2)}) async-start(), calls=%async_computation.5 | async-start | bytes 16711680 | tf_op jit(solution)/shard_map/all_gather | solution.py:71
  9.0 0.6 copy-start.13
  13.4 0.6 copy-start.12
  235.2 3.5 copy-start.4
  235.2 3.6 copy-start.7
  235.2 3.6 copy-start.8
  235.2 3.6 copy-start.14
  235.2 3.6 copy-start.15
  238.8 7.0 copy-start.3
  241.2 15.1 %all-to-all-start.1 = ((bf16[10,16,128]{2,0,1:T(8,128)(2,1)}), bf16[10,16,128]{2,0,1:T(8,128)(2,1)}, u32[]{:S(2)}, u32[]{:S(2)}) async-start(bf16[10,16,128]{2,0,1:T(8,128)(2,1)} %copy.26), calls=%async_computation.1 | async-start | bytes 131072 | tf_op jit(solution)/shard_map/all_to_all | solution.py:82
  256.4 32.3 %all-to-all-start = ((bf16[128,16,192]{0,2,1:T(8,128)(2,1)}), bf16[128,16,192]{0,2,1:T(8,128)(2,1)}, u32[]{:S(2)}, u32[]{:S(2)}) async-start(bf16[128,16,192]{0,2,1:T(8,128)(2,1)} %bitcast.104), calls=%async_computation | async-start | bytes 1572864 | tf_op jit(solution)/shard_map/all_to_all | solution.py:81
  265.5 443.9 %reduce-scatter.2.cloned.1.call-start = ((), (), s32[]{:S(2)}) async-start(), calls=%async_computation.6 | async-start | bytes 6684672 | tf_op jit(solution)/shard_map/reduce_scatter | solution.py:121
  299.0 35.5 %copy-start.6 = (f32[1536]{0:T(1024)S(1)}, f32[1536]{0:T(1024)}, u32[]{:S(2)}) copy-start(f32[1536]{0:T(1024)} %get-tuple-element.60) | copy-start | bytes 18436
  299.0 2.6 copy-start.2
  303.0 2.6 copy-start.2
  307.0 2.6 copy-start.2
  311.1 2.6 copy-start.2
  315.1 22.0 %copy-start.5 = (f32[1536]{0:T(1024)S(1)}, f32[1536]{0:T(1024)}, u32[]{:S(2)}) copy-start(f32[1536]{0:T(1024)} %get-tuple-element.55) | copy-start | bytes 18436
  336.2 0.9 copy-start.1
  493.9 218.5 %copy-start.10 = (f32[1536]{0:T(1024)S(1)}, f32[1536]{0:T(1024)}, u32[]{:S(2)}) copy-start(f32[1536]{0:T(1024)} %get-tuple-element.61) | copy-start | bytes 18436
  493.9 218.5 %copy-start.11 = (f32[1536]{0:T(1024)S(1)}, f32[1536]{0:T(1024)}, u32[]{:S(2)}) copy-start(f32[1536]{0:T(1024)} %get-tuple-element.62) | copy-start | bytes 18436
  493.9 218.5 %copy-start.16 = (bf16[64,1536]{1,0:T(8,128)(2,1)S(1)}, bf16[64,1536]{1,0:T(8,128)(2,1)}, u32[]{:S(2)}) copy-start(bf16[64,1536]{1,0:T(8,128)(2,1)} %param.22) | copy-start | bytes 589828
  493.9 265.6 %copy-start.9 = (f32[1,32,128]{2,1,0:T(8,128)S(1)}, f32[1,32,128]{2,1,0:T(8,128)}, u32[]{:S(2)}) copy-start(f32[1,32,128]{2,1,0:T(8,128)} %param.23) | copy-start | bytes 49156
  714.0 3.8 collective-permute-start
Sparse Core Ops, SparseCore 0:
  10.6 216.2 all-gather.1
  494.0 215.3 reduce-scatter.1
